TPU v7x, 1024 devices: a whole 4x8x16 slice. The times are simulated.
1024 devices in a mesh: row: 16 (over x, y_lo), col: 32 (over z, core), layer: 2 (over y_hi).
Axes of the slice: x: 4, y: 8 (y_hi: 2, y_lo: 4; y = y_hi * 4 + y_lo), z: 16, core: 2. Of those that a mesh axis runs over, the one named last changes fastest.
Arguments:
- tile_data: bfloat16 [16, 32, 3, 128, 128], P('row', 'col'), may hold values from -0.5 to 0.5
- block_rows: int32 [16, 32, 3], P('row', 'col'), may hold values from 0 to 3, as said below
- block_cols: int32 [16, 32, 3], P('row', 'col'), may hold values from 0 to 1
- filled_count: int32 [16, 32], P('row', 'col'), may hold values from 1 to 3, as said below
Outputs:
- product: float32 [8192, 8192], P(('row', 'layer'), 'col')
Inputs may be any that keep to these rules, and one draw needn't show every extreme that they name: `block_rows`: within one grid cell the first filled_count slots name distinct block positions. `filled_count`: some grid cell has all 3 slots filled.
All inputs are finite; a program needn't handle non-finite values.
Results may differ from a plain program's by a relative error of at most 0.0003.
Values may be sent and summed in bfloat16 or wider, within the bound.
A program may use at most 64 MiB of HBM per device.

v0:
```python
import jax
import jax.numpy as jnp
from jax import lax
from jax.sharding import PartitionSpec as P

BC = 2


def as_sent(shard):

    def short(part):
        return part.astype(jnp.bfloat16) if part.dtype == jnp.float32 else part

    return jax.tree.map(short, shard)


def from_behind(block, axis, distance):
    devices = range(lax.axis_size(axis))
    route = [((i - distance) % len(devices), i) for i in devices]
    return lax.ppermute(block, axis, route)


def move_bundle(bundle, offset_by):
    return jax.tree.map(
        lambda part, own: part.astype(own.dtype),
        from_behind(as_sent(bundle), "col", offset_by),
        bundle,
    )


def move_panel(b_panel, offset_by):
    return jax.tree.map(
        lambda part, own: part.astype(own.dtype),
        from_behind(as_sent(b_panel), "row", offset_by),
        b_panel,
    )


def pick_where(chosen_mask, shifted, current):

    def select_leaf(fresh_leaf, stale_leaf):
        shaped = chosen_mask.reshape(
            chosen_mask.shape + (1,) * (fresh_leaf.ndim - chosen_mask.ndim)
        )
        return jnp.where(shaped, fresh_leaf, stale_leaf)

    return jax.tree.map(select_leaf, shifted, current)


def align_bundle(bundle, offsets, axis_length):
    for bit_number in range(axis_length.bit_length() - 1):
        shifted = move_bundle(bundle, -(1 << bit_number))
        bundle = pick_where(offsets // (1 << bit_number) % 2 == 1, shifted, bundle)
    return bundle


def align_panel(b_panel, offset_value, axis_length):
    for bit_number in range(axis_length.bit_length() - 1):
        shifted = move_panel(b_panel, -(1 << bit_number))
        b_panel = pick_where(offset_value // (1 << bit_number) % 2 == 1, shifted, b_panel)
    return b_panel


def spread_panel(b_panel, rows_cell, cols_cell):
    b_tiles, b_rows, b_cols, b_count = b_panel
    slot_count, tile_width = (b_tiles.shape[0], b_tiles.shape[1])
    is_live = jnp.arange(slot_count) < b_count[0]
    row_hits = (b_rows[:, None] == jnp.arange(rows_cell)[None, :]) & is_live[:, None]
    col_hits = b_cols[:, None] == jnp.arange(cols_cell)[None, :]
    placing = (row_hits[:, :, None] & col_hits[:, None, :]).astype(jnp.bfloat16)
    dense_rows = jnp.einsum("skc,sxy->kxcy", placing, b_tiles, preferred_element_type=jnp.float32)
    return dense_rows.astype(jnp.bfloat16).reshape(rows_cell, tile_width, cols_cell * tile_width)


def add_dense(running, bundle, dense_rows, rows_cell, cols_cell):
    a_tiles, a_rows, a_cols, a_count = bundle
    member_count, slot_count, tile_width = (a_tiles.shape[0], a_tiles.shape[1], a_tiles.shape[2])
    inner_index = (jnp.arange(member_count)[:, None] * cols_cell + a_cols).reshape(-1)
    gathered = jnp.take(dense_rows, inner_index, axis=0)
    flat_tiles = a_tiles.reshape(member_count * slot_count, tile_width, tile_width)
    partial_rows = jnp.einsum(
        "sxy,syz->sxz", flat_tiles, gathered, preferred_element_type=jnp.float32
    )
    is_live = (jnp.arange(slot_count)[None, :] < a_count[:, None]).reshape(-1)
    routing = (
        (a_rows.reshape(-1)[:, None] == jnp.arange(rows_cell)[None, :]) & is_live[:, None]
    ).astype(jnp.float32)
    return running + jnp.einsum(
        "si,sxz->ixz", routing, partial_rows, precision=lax.Precision.HIGHEST
    )


def add_every(running, bundle, b_panel, rows_cell, cols_cell):
    dense_rows = spread_panel(b_panel, rows_cell, cols_cell)
    return add_dense(running, bundle, dense_rows, rows_cell, cols_cell)


def combine(running, bundle, b_panel, rows_cell, cols_cell):
    return add_every(running, bundle, b_panel, rows_cell, cols_cell)


def local(tile_data, block_rows, block_cols, filled_count):
    rows_count = lax.axis_size("row")
    cols_count = lax.axis_size("col")
    layer_count = lax.axis_size("layer")
    col_ratio = cols_count // rows_count
    sections = rows_count // layer_count
    row_here = lax.axis_index("row")
    col_here = lax.axis_index("col")
    layer_here = lax.axis_index("layer")
    own_tiles = tile_data[0, 0]
    own_rows = block_rows[0, 0]
    own_cols = block_cols[0, 0]
    own_count = filled_count[0]
    tile_width = own_tiles.shape[-1]
    cols_cell = BC
    rows_cell = col_ratio * cols_cell
    running = jnp.zeros((rows_cell, tile_width, cols_cell * tile_width), jnp.float32)
    middle = 0
    members = jnp.arange(col_ratio)
    offsets = (
        col_ratio * row_here
        + col_ratio * sections * layer_here
        + members
        - col_here % col_ratio
        + col_ratio * middle
    ) % cols_count
    bundle = (
        jnp.broadcast_to(own_tiles[None], (col_ratio,) + own_tiles.shape),
        jnp.broadcast_to(own_rows[None], (col_ratio,) + own_rows.shape),
        jnp.broadcast_to(own_cols[None], (col_ratio,) + own_cols.shape),
        jnp.broadcast_to(own_count, (col_ratio,)),
    )
    bundle = align_bundle(bundle, offsets, cols_count)
    b_panel = (own_tiles, own_rows, own_cols, own_count)
    panel_offset = (col_here // col_ratio + sections * layer_here + middle) % rows_count
    b_panel = align_panel(b_panel, panel_offset, rows_count)
    for section in range(sections):
        running = combine(running, bundle, b_panel, rows_cell, cols_cell)
        if section + 1 < sections:
            bundle = move_bundle(bundle, -col_ratio)
            b_panel = move_panel(b_panel, -1)
    partial_block = running.reshape(rows_cell * tile_width, cols_cell * tile_width)
    return lax.psum_scatter(partial_block, "layer", scatter_dimension=0, tiled=True)


def solution(mesh):
    in_specs = (
        P("row", "col", None, None, None),
        P("row", "col", None),
        P("row", "col", None),
        P("row", "col"),
    )
    out_specs = P(("row", "layer"), "col")
    return jax.shard_map(local, mesh=mesh, in_specs=in_specs, out_specs=out_specs, check_vma=False)
```

profile of v0, /device:TPU:1, one launch (start us, length us, event | category | flops | bytes accessed | tf_op | source)
XLA Modules:
  0.0 627.0 jit_solution(6406439576663794919)
XLA Ops:
  7.5 8.3 %collective-permute-start.15 = (bf16[3,128,128]{2,0,1:T(4,128)(2,1)S(1)}, bf16[3,128,128]{2,0,1:T(4,128)(2,1)S(1)}, u32[]{:S(2)}, u32[]{:S(2)}) collective-permute-start(bf16[3,128,128]{2,0,1:T(4,128)(2,1)S(1)} %bitcast.164), channel_id=1, source_target_pairs={{64,0},{128,64},{192,128},{256,192},{320,256},{384,320},{448,384},... | collective-permute-start | bytes 294920 | tf_op jit(solution)/shard_map/ppermute | solution.py:20
  15.8 7.8 %collective-permute-start.10 = (bf16[2,3,128,128]{3,2,1,0:T(8,128)(2,1)S(1)}, bf16[2,3,128,128]{3,2,1,0:T(8,128)(2,1)S(1)}, u32[]{:S(2)}, u32[]{:S(2)}) collective-permute-start(bf16[2,3,128,128]{3,2,1,0:T(8,128)(2,1)S(1)} %broadcast_in_dim.267), channel_id=1, source_target_pairs={{2,0},{4,2},{6,4},{8,6},{10,8},{12,10},{14,12},{16,14},{18,16},{20... | collective-permute-start | bytes 589832 | tf_op jit(solution)/shard_map/ppermute | solution.py:20
  24.3 8.6 %collective-permute-start.5 = (s32[2]{0:T(128)S(1)}, s32[2]{0:T(128)S(1)}, u32[]{:S(2)}, u32[]{:S(2)}) collective-permute-start(s32[2]{0:T(128)S(1)} %broadcast_in_dim.260), channel_id=1, source_target_pairs={{2,0},{4,2},{6,4},{8,6},{10,8},{12,10},{14,12},{16,14},{18,16},{20... | collective-permute-start | bytes 32 | tf_op jit(solution)/shard_map/ppermute | solution.py:20
  45.2 8.1 %collective-permute-start.19 = (s32[3]{0:T(128)S(1)}, s32[3]{0:T(128)S(1)}, u32[]{:S(2)}, u32[]{:S(2)}) collective-permute-start(s32[3]{0:T(128)S(1)} %bitcast.175), channel_id=1, source_target_pairs={{64,0},{128,64},{192,128},{256,192},{320,256},{384,320},{448,384},... | collective-permute-start | bytes 44 | tf_op jit(solution)/shard_map/ppermute | solution.py:20
  83.7 6.7 %collective-permute-start.49 = (s32[1]{0:T(128)}, s32[1]{0:T(128)}, u32[]{:S(2)}, u32[]{:S(2)}) collective-permute-start(s32[1]{0:T(128)} %collective-permute-done.41), channel_id=1, source_target_pairs={{64,0},{128,64},{192,128},{256,192},{320,256},{384,320},{448,384},... | collective-permute-start | bytes 20 | tf_op jit(solution)/shard_map/ppermute | solution.py:20
  107.3 11.2 %collective-permute-start.57 = (s32[1]{0:T(128)}, s32[1]{0:T(128)}, u32[]{:S(2)}, u32[]{:S(2)}) collective-permute-start(s32[1]{0:T(128)} %collective-permute-done.49), channel_id=1, source_target_pairs={{64,0},{128,64},{192,128},{256,192},{320,256},{384,320},{448,384},... | collective-permute-start | bytes 20 | tf_op jit(solution)/shard_map/ppermute | solution.py:20
  119.8 7.4 %collective-permute-start.65 = (s32[1]{0:T(128)}, s32[1]{0:T(128)}, u32[]{:S(2)}, u32[]{:S(2)}) collective-permute-start(s32[1]{0:T(128)} %collective-permute-done.57), channel_id=1, source_target_pairs={{64,0},{128,64},{192,128},{256,192},{320,256},{384,320},{448,384},... | collective-permute-start | bytes 20 | tf_op jit(solution)/shard_map/ppermute | solution.py:20
  130.6 7.4 %collective-permute-start.73 = (s32[1]{0:T(128)}, s32[1]{0:T(128)}, u32[]{:S(2)}, u32[]{:S(2)}) collective-permute-start(s32[1]{0:T(128)} %collective-permute-done.65), channel_id=1, source_target_pairs={{64,0},{128,64},{192,128},{256,192},{320,256},{384,320},{448,384},... | collective-permute-start | bytes 20 | tf_op jit(solution)/shard_map/ppermute | solution.py:20
  145.9 7.4 %collective-permute-start.81 = (s32[1]{0:T(128)}, s32[1]{0:T(128)}, u32[]{:S(2)}, u32[]{:S(2)}) collective-permute-start(s32[1]{0:T(128)} %collective-permute-done.73), channel_id=1, source_target_pairs={{64,0},{128,64},{192,128},{256,192},{320,256},{384,320},{448,384},... | collective-permute-start | bytes 20 | tf_op jit(solution)/shard_map/ppermute | solution.py:20
  154.1 6.2 collective-permute-start.9
  167.1 7.4 %collective-permute-start.89 = (s32[1]{0:T(128)}, s32[1]{0:T(128)}, u32[]{:S(2)}, u32[]{:S(2)}) collective-permute-start(s32[1]{0:T(128)} %collective-permute-done.81), channel_id=1, source_target_pairs={{64,0},{128,64},{192,128},{256,192},{320,256},{384,320},{448,384},... | collective-permute-start | bytes 20 | tf_op jit(solution)/shard_map/ppermute | solution.py:20
  191.1 7.4 %collective-permute-start.42 = (s32[3]{0:T(128)S(1)}, s32[3]{0:T(128)S(1)}, u32[]{:S(2)}, u32[]{:S(2)}) collective-permute-start(s32[3]{0:T(128)S(1)} %broadcast_select_fusion.25), channel_id=1, source_target_pairs={{64,0},{128,64},{192,128},{256,192},{320,256},{384,320},{448,384},... | collective-permute-start | bytes 44 | tf_op jit(solution)/shard_map/ppermute | solution.py:20
  230.3 7.9 %collective-permute-start.3 = (s32[2,3]{1,0:T(2,128)S(1)}, s32[2,3]{1,0:T(2,128)S(1)}, u32[]{:S(2)}, u32[]{:S(2)}) collective-permute-start(s32[2,3]{1,0:T(2,128)S(1)} %get-tuple-element.31), channel_id=1, source_target_pairs={{16,0},{18,2},{20,4},{22,6},{24,8},{26,10},{28,12},{30,14},{32,16}... | collective-permute-start | bytes 80 | tf_op jit(solution)/shard_map/ppermute | solution.py:20
  264.7 7.5 %collective-permute-start.66 = (s32[3]{0:T(128)S(1)}, s32[3]{0:T(128)S(1)}, u32[]{:S(2)}, u32[]{:S(2)}) collective-permute-start(s32[3]{0:T(128)S(1)} %collective-permute-done.58), channel_id=1, source_target_pairs={{64,0},{128,64},{192,128},{256,192},{320,256},{384,320},{448,384},... | collective-permute-start | bytes 44 | tf_op jit(solution)/shard_map/ppermute | solution.py:20
  278.6 10.3 %collective-permute-start.4 = (s32[2,3]{1,0:T(2,128)S(1)}, s32[2,3]{1,0:T(2,128)S(1)}, u32[]{:S(2)}, u32[]{:S(2)}) collective-permute-start(s32[2,3]{1,0:T(2,128)S(1)} %get-tuple-element.29), channel_id=1, source_target_pairs={{32,0},{34,2},{36,4},{38,6},{40,8},{42,10},{44,12},{46,14},{48,16}... | collective-permute-start | bytes 80 | tf_op jit(solution)/shard_map/ppermute | solution.py:20
  299.8 7.5 %collective-permute-start.82 = (s32[3]{0:T(128)S(1)}, s32[3]{0:T(128)S(1)}, u32[]{:S(2)}, u32[]{:S(2)}) collective-permute-start(s32[3]{0:T(128)S(1)} %collective-permute-done.74), channel_id=1, source_target_pairs={{64,0},{128,64},{192,128},{256,192},{320,256},{384,320},{448,384},... | collective-permute-start | bytes 44 | tf_op jit(solution)/shard_map/ppermute | solution.py:20
  320.9 7.5 %collective-permute-start.88 = (s32[3]{0:T(128)S(1)}, s32[3]{0:T(128)S(1)}, u32[]{:S(2)}, u32[]{:S(2)}) collective-permute-start(s32[3]{0:T(128)S(1)} %collective-permute-done.80), channel_id=1, source_target_pairs={{64,0},{128,64},{192,128},{256,192},{320,256},{384,320},{448,384},... | collective-permute-start | bytes 44 | tf_op jit(solution)/shard_map/ppermute | solution.py:20
  392.9 9.4 %collective-permute-start.39 = (bf16[3,128,128]{2,0,1:T(4,128)(2,1)S(1)}, bf16[3,128,128]{2,0,1:T(4,128)(2,1)S(1)}, u32[]{:S(2)}, u32[]{:S(2)}) collective-permute-start(bf16[3,128,128]{2,0,1:T(4,128)(2,1)S(1)} %broadcast_select_fusion.8), channel_id=1, source_target_pairs={{64,0},{128,64},{192,128},{256,192},{320,256},{384,320},{448,384},... | collective-permute-start | bytes 294920 | tf_op jit(solution)/shard_map/ppermute | solution.py:20
  405.4 7.7 %collective-permute-start.47 = (bf16[3,128,128]{2,0,1:T(4,128)(2,1)S(1)}, bf16[3,128,128]{2,0,1:T(4,128)(2,1)S(1)}, u32[]{:S(2)}, u32[]{:S(2)}) collective-permute-start(bf16[3,128,128]{2,0,1:T(4,128)(2,1)S(1)} %collective-permute-done.39), channel_id=1, source_target_pairs={{64,0},{128,64},{192,128},{256,192},{320,256},{384,320},{448,384},... | collective-permute-start | bytes 294920 | tf_op jit(solution)/shard_map/ppermute | solution.py:20
  426.3 7.2 %collective-permute-start.63 = (bf16[3,128,128]{2,0,1:T(4,128)(2,1)S(1)}, bf16[3,128,128]{2,0,1:T(4,128)(2,1)S(1)}, u32[]{:S(2)}, u32[]{:S(2)}) collective-permute-start(bf16[3,128,128]{2,0,1:T(4,128)(2,1)S(1)} %collective-permute-done.55), channel_id=1, source_target_pairs={{64,0},{128,64},{192,128},{256,192},{320,256},{384,320},{448,384},... | collective-permute-start | bytes 294920 | tf_op jit(solution)/shard_map/ppermute | solution.py:20
  433.6 7.4 %collective-permute-start.14 = (bf16[2,3,128,128]{3,2,1,0:T(8,128)(2,1)S(1)}, bf16[2,3,128,128]{3,2,1,0:T(8,128)(2,1)S(1)}, u32[]{:S(2)}, u32[]{:S(2)}) collective-permute-start(bf16[2,3,128,128]{3,2,1,0:T(8,128)(2,1)S(1)} %broadcast_select_fusion.3), channel_id=1, source_target_pairs={{32,0},{34,2},{36,4},{38,6},{40,8},{42,10},{44,12},{46,14},{48,16}... | collective-permute-start | bytes 589832 | tf_op jit(solution)/shard_map/ppermute | solution.py:20
  447.9 6.4 %collective-permute-start.79 = (bf16[3,128,128]{2,0,1:T(4,128)(2,1)S(1)}, bf16[3,128,128]{2,0,1:T(4,128)(2,1)}, u32[]{:S(2)}, u32[]{:S(2)}) collective-permute-start(bf16[3,128,128]{2,0,1:T(4,128)(2,1)S(1)} %collective-permute-done.71), channel_id=1, source_target_pairs={{64,0},{128,64},{192,128},{256,192},{320,256},{384,320},{448,384},... | collective-permute-start | bytes 294920 | tf_op jit(solution)/shard_map/ppermute | solution.py:20
  476.5 6.5 %collective-permute-done.46 = bf16[2,3,128,128]{3,2,1,0:T(8,128)(2,1)S(1)} collective-permute-done((bf16[2,3,128,128]{3,2,1,0:T(8,128)(2,1)}, bf16[2,3,128,128]{3,2,1,0:T(8,128)(2,1)S(1)}, u32[]{:S(2)}, u32[]{:S(2)}) %collective-permute-start.46) | collective-permute-done | bytes 196640 | tf_op jit(solution)/shard_map/ppermute | solution.py:20
  531.3 88.8 %reduce-scatter.2.cloned.1.call-done = f32[256,256]{1,0:T(8,128)} async-done(((f32[512,256]{1,0:T(8,128)}), f32[256,256]{1,0:T(8,128)}) %reduce-scatter.2.cloned.1.call-update) | async-done | bytes 262160 | tf_op jit(solution)/shard_map/reduce_scatter | solution.py:144
  (363 shorter events, 340.3 us)
Async XLA Ops:
  6.5 613.6 %reduce-scatter.2.cloned.1.call-start = ((), (), s32[]{:S(2)}) async-start(), calls=%async_computation.1 | async-start | bytes 786432 | tf_op jit(solution)/shard_map/reduce_scatter | solution.py:144
  7.5 364.1 %collective-permute-start.15 = (bf16[3,128,128]{2,0,1:T(4,128)(2,1)S(1)}, bf16[3,128,128]{2,0,1:T(4,128)(2,1)S(1)}, u32[]{:S(2)}, u32[]{:S(2)}) collective-permute-start(bf16[3,128,128]{2,0,1:T(4,128)(2,1)S(1)} %bitcast.164), channel_id=1, source_target_pairs={{64,0},{128,64},{192,128},{256,192},{320,256},{384,320},{448,384},... | collective-permute-start | bytes 294920 | tf_op jit(solution)/shard_map/ppermute | solution.py:20
  15.8 364.5 %collective-permute-start.10 = (bf16[2,3,128,128]{3,2,1,0:T(8,128)(2,1)S(1)}, bf16[2,3,128,128]{3,2,1,0:T(8,128)(2,1)S(1)}, u32[]{:S(2)}, u32[]{:S(2)}) collective-permute-start(bf16[2,3,128,128]{3,2,1,0:T(8,128)(2,1)S(1)} %broadcast_in_dim.267), channel_id=1, source_target_pairs={{2,0},{4,2},{6,4},{8,6},{10,8},{12,10},{14,12},{16,14},{18,16},{20... | collective-permute-start | bytes 589832 | tf_op jit(solution)/shard_map/ppermute | solution.py:20
  24.3 29.6 %collective-permute-start.5 = (s32[2]{0:T(128)S(1)}, s32[2]{0:T(128)S(1)}, u32[]{:S(2)}, u32[]{:S(2)}) collective-permute-start(s32[2]{0:T(128)S(1)} %broadcast_in_dim.260), channel_id=1, source_target_pairs={{2,0},{4,2},{6,4},{8,6},{10,8},{12,10},{14,12},{16,14},{18,16},{20... | collective-permute-start | bytes 32 | tf_op jit(solution)/shard_map/ppermute | solution.py:20
  33.0 31.2 %collective-permute-start.27 = (s32[3]{0:T(128)S(1)}, s32[3]{0:T(128)S(1)}, u32[]{:S(2)}, u32[]{:S(2)}) collective-permute-start(s32[3]{0:T(128)S(1)} %bitcast.172), channel_id=1, source_target_pairs={{64,0},{128,64},{192,128},{256,192},{320,256},{384,320},{448,384},... | collective-permute-start | bytes 44 | tf_op jit(solution)/shard_map/ppermute | solution.py:20
  45.2 19.1 %collective-permute-start.19 = (s32[3]{0:T(128)S(1)}, s32[3]{0:T(128)S(1)}, u32[]{:S(2)}, u32[]{:S(2)}) collective-permute-start(s32[3]{0:T(128)S(1)} %bitcast.175), channel_id=1, source_target_pairs={{64,0},{128,64},{192,128},{256,192},{320,256},{384,320},{448,384},... | collective-permute-start | bytes 44 | tf_op jit(solution)/shard_map/ppermute | solution.py:20
  58.2 46.8 %collective-permute-start = (s32[2,3]{1,0:T(2,128)S(1)}, s32[2,3]{1,0:T(2,128)S(1)}, u32[]{:S(2)}, u32[]{:S(2)}) collective-permute-start(s32[2,3]{1,0:T(2,128)S(1)} %broadcast_in_dim.258), channel_id=1, source_target_pairs={{2,0},{4,2},{6,4},{8,6},{10,8},{12,10},{14,12},{16,14},{18,16},{20... | collective-permute-start | bytes 80 | tf_op jit(solution)/shard_map/ppermute | solution.py:20
  64.2 43.1 %collective-permute-start.31 = (s32[2,3]{1,0:T(2,128)S(1)}, s32[2,3]{1,0:T(2,128)S(1)}, u32[]{:S(2)}, u32[]{:S(2)}) collective-permute-start(s32[2,3]{1,0:T(2,128)S(1)} %broadcast_in_dim.276), channel_id=1, source_target_pairs={{2,0},{4,2},{6,4},{8,6},{10,8},{12,10},{14,12},{16,14},{18,16},{20... | collective-permute-start | bytes 80 | tf_op jit(solution)/shard_map/ppermute | solution.py:20
  101.5 29.0 %collective-permute-start.8 = (s32[2]{0:T(128)S(1)}, s32[2]{0:T(128)S(1)}, u32[]{:S(2)}, u32[]{:S(2)}) collective-permute-start(s32[2]{0:T(128)S(1)} %get-tuple-element.10), channel_id=1, source_target_pairs={{16,0},{18,2},{20,4},{22,6},{24,8},{26,10},{28,12},{30,14},{32,16}... | collective-permute-start | bytes 32 | tf_op jit(solution)/shard_map/ppermute | solution.py:20
  104.9 39.0 %collective-permute-start.29 = (s32[3]{0:T(128)S(1)}, s32[3]{0:T(128)S(1)}, u32[]{:S(2)}, u32[]{:S(2)}) collective-permute-start(s32[3]{0:T(128)S(1)} %broadcast_select_fusion.21), channel_id=1, source_target_pairs={{256,0},{320,64},{384,128},{448,192},{512,256},{576,320},{640,384}... | collective-permute-start | bytes 44 | tf_op jit(solution)/shard_map/ppermute | solution.py:20
  128.0 17.9 %collective-permute-start.21 = (s32[3]{0:T(128)S(1)}, s32[3]{0:T(128)S(1)}, u32[]{:S(2)}, u32[]{:S(2)}) collective-permute-start(s32[3]{0:T(128)S(1)} %broadcast_select_fusion.22), channel_id=1, source_target_pairs={{256,0},{320,64},{384,128},{448,192},{512,256},{576,320},{640,384}... | collective-permute-start | bytes 44 | tf_op jit(solution)/shard_map/ppermute | solution.py:20
  138.8 59.8 %collective-permute-start.1 = (s32[2,3]{1,0:T(2,128)S(1)}, s32[2,3]{1,0:T(2,128)S(1)}, u32[]{:S(2)}, u32[]{:S(2)}) collective-permute-start(s32[2,3]{1,0:T(2,128)S(1)} %get-tuple-element.35), channel_id=1, source_target_pairs={{4,0},{6,2},{8,4},{10,6},{12,8},{14,10},{16,12},{18,14},{20,16},{2... | collective-permute-start | bytes 80 | tf_op jit(solution)/shard_map/ppermute | solution.py:20
  144.0 56.6 %collective-permute-start.32 = (s32[2,3]{1,0:T(2,128)S(1)}, s32[2,3]{1,0:T(2,128)S(1)}, u32[]{:S(2)}, u32[]{:S(2)}) collective-permute-start(s32[2,3]{1,0:T(2,128)S(1)} %get-tuple-element.36), channel_id=1, source_target_pairs={{4,0},{6,2},{8,4},{10,6},{12,8},{14,10},{16,12},{18,14},{20,16},{2... | collective-permute-start | bytes 80 | tf_op jit(solution)/shard_map/ppermute | solution.py:20
  204.8 18.7 %collective-permute-start.2 = (s32[2,3]{1,0:T(2,128)S(1)}, s32[2,3]{1,0:T(2,128)S(1)}, u32[]{:S(2)}, u32[]{:S(2)}) collective-permute-start(s32[2,3]{1,0:T(2,128)S(1)} %get-tuple-element.33), channel_id=1, source_target_pairs={{8,0},{10,2},{12,4},{14,6},{16,8},{18,10},{20,12},{22,14},{24,16},... | collective-permute-start | bytes 80 | tf_op jit(solution)/shard_map/ppermute | solution.py:20
  225.4 18.0 %collective-permute-start.69 = (s32[2]{0:T(128)S(1)}, s32[2]{0:T(128)S(1)}, u32[]{:S(2)}, u32[]{:S(2)}) collective-permute-start(s32[2]{0:T(128)S(1)} %collective-permute-done.61), channel_id=1, source_target_pairs={{4,0},{6,2},{8,4},{10,6},{12,8},{14,10},{16,12},{18,14},{20,16},{2... | collective-permute-start | bytes 32 | tf_op jit(solution)/shard_map/ppermute | solution.py:20
  230.3 42.6 %collective-permute-start.3 = (s32[2,3]{1,0:T(2,128)S(1)}, s32[2,3]{1,0:T(2,128)S(1)}, u32[]{:S(2)}, u32[]{:S(2)}) collective-permute-start(s32[2,3]{1,0:T(2,128)S(1)} %get-tuple-element.31), channel_id=1, source_target_pairs={{16,0},{18,2},{20,4},{22,6},{24,8},{26,10},{28,12},{30,14},{32,16}... | collective-permute-start | bytes 80 | tf_op jit(solution)/shard_map/ppermute | solution.py:20
  238.3 36.6 %collective-permute-start.34 = (s32[2,3]{1,0:T(2,128)S(1)}, s32[2,3]{1,0:T(2,128)S(1)}, u32[]{:S(2)}, u32[]{:S(2)}) collective-permute-start(s32[2,3]{1,0:T(2,128)S(1)} %get-tuple-element.32), channel_id=1, source_target_pairs={{16,0},{18,2},{20,4},{22,6},{24,8},{26,10},{28,12},{30,14},{32,16}... | collective-permute-start | bytes 80 | tf_op jit(solution)/shard_map/ppermute | solution.py:20
  274.9 32.3 %collective-permute-start.35 = (s32[2,3]{1,0:T(2,128)S(1)}, s32[2,3]{1,0:T(2,128)S(1)}, u32[]{:S(2)}, u32[]{:S(2)}) collective-permute-start(s32[2,3]{1,0:T(2,128)S(1)} %get-tuple-element.30), channel_id=1, source_target_pairs={{32,0},{34,2},{36,4},{38,6},{40,8},{42,10},{44,12},{46,14},{48,16}... | collective-permute-start | bytes 80 | tf_op jit(solution)/shard_map/ppermute | solution.py:20
  278.6 30.6 %collective-permute-start.4 = (s32[2,3]{1,0:T(2,128)S(1)}, s32[2,3]{1,0:T(2,128)S(1)}, u32[]{:S(2)}, u32[]{:S(2)}) collective-permute-start(s32[2,3]{1,0:T(2,128)S(1)} %get-tuple-element.29), channel_id=1, source_target_pairs={{32,0},{34,2},{36,4},{38,6},{40,8},{42,10},{44,12},{46,14},{48,16}... | collective-permute-start | bytes 80 | tf_op jit(solution)/shard_map/ppermute | solution.py:20
  309.5 20.2 %collective-permute-start.36 = (s32[2,3]{1,0:T(2,128)S(1)}, s32[2,3]{1,0:T(2,128)S(1)}, u32[]{:S(2)}, u32[]{:S(2)}) collective-permute-start(s32[2,3]{1,0:T(2,128)S(1)} %get-tuple-element.28), channel_id=1, source_target_pairs={{4,0},{6,2},{8,4},{10,6},{12,8},{14,10},{16,12},{18,14},{20,16},{2... | collective-permute-start | bytes 80 | tf_op jit(solution)/shard_map/ppermute | solution.py:20
  314.3 18.0 %collective-permute-start.43 = (s32[2,3]{1,0:T(2,128)S(1)}, s32[2,3]{1,0:T(2,128)S(1)}, u32[]{:S(2)}, u32[]{:S(2)}) collective-permute-start(s32[2,3]{1,0:T(2,128)S(1)} %get-tuple-element.20), channel_id=1, source_target_pairs={{4,0},{6,2},{8,4},{10,6},{12,8},{14,10},{16,12},{18,14},{20,16},{2... | collective-permute-start | bytes 80 | tf_op jit(solution)/shard_map/ppermute | solution.py:20
  388.3 24.8 %collective-permute-start.12 = (bf16[2,3,128,128]{3,2,1,0:T(8,128)(2,1)S(1)}, bf16[2,3,128,128]{3,2,1,0:T(8,128)(2,1)S(1)}, u32[]{:S(2)}, u32[]{:S(2)}) collective-permute-start(bf16[2,3,128,128]{3,2,1,0:T(8,128)(2,1)S(1)} %broadcast_select_fusion.1), channel_id=1, source_target_pairs={{8,0},{10,2},{12,4},{14,6},{16,8},{18,10},{20,12},{22,14},{24,16},... | collective-permute-start | bytes 589832 | tf_op jit(solution)/shard_map/ppermute | solution.py:20
  413.2 20.3 %collective-permute-start.13 = (bf16[2,3,128,128]{3,2,1,0:T(8,128)(2,1)S(1)}, bf16[2,3,128,128]{3,2,1,0:T(8,128)(2,1)S(1)}, u32[]{:S(2)}, u32[]{:S(2)}) collective-permute-start(bf16[2,3,128,128]{3,2,1,0:T(8,128)(2,1)S(1)} %broadcast_select_fusion.2), channel_id=1, source_target_pairs={{16,0},{18,2},{20,4},{22,6},{24,8},{26,10},{28,12},{30,14},{32,16}... | collective-permute-start | bytes 589832 | tf_op jit(solution)/shard_map/ppermute | solution.py:20
  433.6 20.7 %collective-permute-start.14 = (bf16[2,3,128,128]{3,2,1,0:T(8,128)(2,1)S(1)}, bf16[2,3,128,128]{3,2,1,0:T(8,128)(2,1)S(1)}, u32[]{:S(2)}, u32[]{:S(2)}) collective-permute-start(bf16[2,3,128,128]{3,2,1,0:T(8,128)(2,1)S(1)} %broadcast_select_fusion.3), channel_id=1, source_target_pairs={{32,0},{34,2},{36,4},{38,6},{40,8},{42,10},{44,12},{46,14},{48,16}... | collective-permute-start | bytes 589832 | tf_op jit(solution)/shard_map/ppermute | solution.py:20
  (91 other events, 785.9 us)
Sparse Core Ops, SparseCore 0:
  531.4 88.6 reduce-scatter.1
where the time goes:
time: 630 us; the launch traced here: 627 us
  starting transfers between devices  395 us (63%)
  waiting for transfers between devices  166 us (26%)
  local copies, waits for them, and re-layouts  19.4 us (3%)
  between operations  18.6 us (3%)
  matrix products  16.7 us (3%)
  other arithmetic  11 us (2%)
    ppermute x92, starting transfers between devices, from_behind(): return lax.ppermute(block, axis, route)  395 us
    reduce_scatter x1, waiting for transfers between devices, local(): lax.psum_scatter(partial_block, 'layer', scatter_dimension=0, tiled=True)  88.8 us
    ppermute x92, waiting for transfers between devices, from_behind(): return lax.ppermute(block, axis, route)  77.5 us
  transfers between devices with their start and end apart: 93, of which 46 were waited for; matrix products, arithmetic and copies ran while one was open for 6% of the time, Pallas kernels for 0%

commit v1 on v0

v1 whole, which is shorter than its diff:
```python
import functools

import jax
import jax.numpy as jnp
from jax import lax
from jax.experimental import pallas as pl
from jax.experimental.pallas import tpu as pltpu
from jax.sharding import PartitionSpec as P

TILE = 128
SLOTS = 3
NX, NY, NZ = 4, 8, 16
Y_LO = 4
N_ROW = 16
N_COL = 32
MARK = 16
ROWS = SLOTS * TILE + MARK
CHUNKS = ((0, 128), (128, 128), (256, 144))
FIRST, SECOND = (0, 208), (208, 192)
MESH = pl.DeviceIdType.MESH


def kernel(
    rows_ref, cols_ref, count_ref, tiles_ref, out_ref,
    left, right, own_sem,
    ring_s, ring_r, far_s, far_r, twin_s, twin_r, grid_s, grid_r,
):
    row = lax.axis_index("row")
    col = lax.axis_index("col")
    layer = lax.axis_index("layer")
    x, y = row // Y_LO, layer * Y_LO + row % Y_LO
    z, core = col // 2, col % 2
    fx, fy, gx, gy = 1 - core, core, core, 1 - core
    away = 1 - 2 * core

    def at_xy(dx, dy):
        nx, ny = (x + dx + NX) % NX, (y + dy + NY) % NY
        return (nx * Y_LO + ny % Y_LO, col, ny // Y_LO)

    def at_z(dz):
        return (row, ((z + dz + NZ) % NZ) * 2 + core, layer)

    twin = (row, z * 2 + 1 - core, layer)

    def left_slot(dz, own):
        return ((z + dz + NZ) % NZ) * 2 + (core if own else 1 - core)

    def right_slot(f, g):
        cx = (x + f * fx + g * gx + NX) % NX
        cy = (y + f * fy + g * gy + NY) % Y_LO
        return cx * Y_LO + cy

    def remote(ref, slot, span, send, recv, device):
        part = ref.at[slot, pl.ds(span[0], span[1])]
        return pltpu.make_async_remote_copy(
            src_ref=part, dst_ref=part, send_sem=send, recv_sem=recv,
            device_id=device, device_id_type=MESH,
        )

    whole = (0, ROWS)

    def ring(way, dist, k):
        w = 0 if way > 0 else 1
        return remote(
            left, left_slot(-way * dist, True), CHUNKS[k],
            ring_s.at[w, dist, k], ring_r.at[w, dist, k], at_z(way),
        )

    def ring_in(way, dist, k):
        w = 0 if way > 0 else 1
        return remote(
            left, left_slot(-way * dist, True), CHUNKS[k],
            ring_s.at[w, dist - 1, k], ring_r.at[w, dist - 1, k], at_z(way),
        )

    def far(k):
        return remote(left, left_slot(-7 * away, True), CHUNKS[k], far_s.at[k], far_r.at[k], at_z(away))

    def far_in(k):
        return remote(left, left_slot(8, True), CHUNKS[k], far_s.at[k], far_r.at[k], at_z(away))

    def to_twin(dz, m, k):
        return remote(left, left_slot(dz, True), CHUNKS[k], twin_s.at[m, k], twin_r.at[m, k], twin)

    def from_twin(dz, m, k):
        return remote(left, left_slot(dz, False), CHUNKS[k], twin_s.at[m, k], twin_r.at[m, k], twin)

    def along(n, f, g, span, first, way):
        step = way if first else 0
        dev = at_xy(way * fx, way * fy) if first else at_xy(way * gx, way * gy)
        return remote(right, right_slot(f, g), span, grid_s.at[n], grid_r.at[n], dev)

    moves = {}
    moves[0] = (0, 0, whole, True, 1)
    moves[1] = (0, 0, whole, True, -1)
    moves[2] = (-1, 0, FIRST, True, 1)
    moves[3] = (1, 0, SECOND, True, -1)
    for i, f in enumerate((0, -1, 1, 2)):
        moves[4 + 4 * i] = (f, 0, whole, False, 1)
        moves[5 + 4 * i] = (f, 0, whole, False, -1)
        moves[6 + 4 * i] = (f, -1, FIRST, False, 1)
        moves[7 + 4 * i] = (f, 1, SECOND, False, -1)

    def go(n):
        along(n, *moves[n]).start()

    def come(n):
        f, g, span, first, way = moves[n]
        if first:
            along(n, f - way, g, span, first, way).wait_recv()
        else:
            along(n, f, g - way, span, first, way).wait_recv()

    def add(m, q):
        half = (m + 1) // 2
        dz = jnp.where(m % 2 == 0, half, -half)
        r = (z + dz + NZ) % NZ
        lslot = r * 2 + q

        def picked(ref, slot, codes):
            marks = ref[slot, pl.ds(SLOTS * TILE, MARK), :].astype(jnp.float32)
            tiles = [ref[slot, pl.ds(s * TILE, TILE), :] for s in range(SLOTS)]
            result = []
            for code in codes:
                total = None
                for s in range(SLOTS):
                    hit = jnp.where(marks[s:s + 1, :] == code, 1.0, 0.0).astype(jnp.bfloat16)
                    term = tiles[s] * hit
                    total = term if total is None else total + term
                result.append(total)
            return result

        base = (4 * layer).astype(jnp.float32)
        a = picked(left, lslot, [base + i for i in range(4)])
        b = picked(right, r, [float(4 * q + i) for i in range(4)])
        lhs = jnp.concatenate([jnp.concatenate(a[:2], axis=1), jnp.concatenate(a[2:], axis=1)], axis=0)
        rhs = jnp.concatenate([jnp.concatenate(b[:2], axis=1), jnp.concatenate(b[2:], axis=1)], axis=0)
        out_ref[...] += jnp.dot(lhs, rhs, preferred_element_type=jnp.float32)

    def add_range(lo, hi):
        def body(m, carry):
            half = (m + 1) // 2
            dz = jnp.where(m % 2 == 0, half, -half)
            for k in range(3):
                from_twin(dz, m, k).wait_recv()
            add(m, 0)
            add(m, 1)
            return carry
        lax.fori_loop(lo, hi, body, 0)

    own = []
    for s in range(2):
        ref, slot = ((left, left_slot(0, True)), (right, right_slot(0, 0)))[s]
        own.append(pltpu.make_async_copy(tiles_ref, ref.at[slot, pl.ds(0, SLOTS * TILE)], own_sem.at[s]))
    for copy in own:
        copy.start()
    barrier = pltpu.get_barrier_semaphore()
    greeted = [at_z(1), at_z(-1), twin, at_xy(1, 0), at_xy(-1, 0), at_xy(0, 1), at_xy(0, -1)]
    for device in greeted:
        pl.semaphore_signal(barrier, inc=1, device_id=device, device_id_type=MESH)
    place = lax.broadcasted_iota(jnp.int32, (MARK, TILE), 0)
    marks = jnp.full((MARK, TILE), -1.0, jnp.float32)
    for s in range(SLOTS):
        code = jnp.where(s < count_ref[0, 0], rows_ref[0, 0, s] * 2 + cols_ref[0, 0, s], -1)
        marks = jnp.where(place == s, code.astype(jnp.float32), marks)
    marks = marks.astype(jnp.bfloat16)
    left[left_slot(0, True), pl.ds(SLOTS * TILE, MARK), :] = marks
    right[right_slot(0, 0), pl.ds(SLOTS * TILE, MARK), :] = marks
    out_ref[...] = jnp.zeros_like(out_ref)
    for copy in own:
        copy.wait()
    pl.semaphore_wait(barrier, len(greeted))

    for k in range(3):
        ring(1, 0, k).start()
        ring(-1, 0, k).start()
    for n in (0, 1, 4, 5):
        go(n)
    for k in range(3):
        to_twin(0, 0, k).start()

    def step_xy(d):
        if d == 1:
            come(0); go(2); go(8); go(9)
            come(1); go(3); go(12); go(13)
            come(4); go(6)
            come(5); go(7)
        elif d == 2:
            come(2); come(3); go(16); go(17)
        elif d == 3:
            come(8); go(10); come(9); go(11)
            come(12); go(14); come(13); go(15)
        elif d == 4:
            come(16); go(18); come(17); go(19)
        elif d == 5:
            for n in (6, 7, 10, 11, 14, 15, 18, 19):
                come(n)

    work = {
        (5, 0): (0, 2), (5, 1): (2, 4), (5, 2): (4, 6),
        (6, 0): (6, 8), (6, 1): (8, 10), (6, 2): (10, 11),
        (7, 0): (11, 12), (7, 1): (12, 13),
    }
    for d in range(1, 8):
        for k in range(3):
            for way in (1, -1):
                ring_in(way, d, k).wait_recv()
                if d < 7:
                    ring(way, d, k).start()
                to_twin(-way * d, 2 * d - 1 if way > 0 else 2 * d, k).start()
            if d == 7:
                far(k).start()
            if k == 0:
                step_xy(d)
            if (d, k) in work:
                add_range(*work[d, k])
    add_range(13, 15)
    for k in range(3):
        far_in(k).wait_recv()
        to_twin(8, 15, k).start()
    add_range(15, 16)

    for k in range(3):
        for d in range(7):
            for way in (1, -1):
                ring(way, d, k).wait_send()
        far(k).wait_send()
        for m in range(16):
            half = (m + 1) // 2
            to_twin(half if m % 2 == 0 else -half, m, k).wait_send()
    for n in moves:
        along(n, *moves[n]).wait_send()


def local(tile_data, block_rows, block_cols, filled_count):
    tiles = tile_data.reshape(SLOTS * TILE, TILE)
    smem = pl.BlockSpec(memory_space=pltpu.SMEM)
    return pl.pallas_call(
        kernel,
        out_shape=jax.ShapeDtypeStruct((2 * TILE, 2 * TILE), jnp.float32),
        in_specs=[smem, smem, smem, pl.BlockSpec(memory_space=pl.ANY)],
        out_specs=pl.BlockSpec(memory_space=pltpu.VMEM),
        scratch_shapes=[
            pltpu.VMEM((N_COL, ROWS, TILE), jnp.bfloat16),
            pltpu.VMEM((N_ROW, ROWS, TILE), jnp.bfloat16),
            pltpu.SemaphoreType.DMA((2,)),
            pltpu.SemaphoreType.DMA((2, 7, 3)),
            pltpu.SemaphoreType.DMA((2, 7, 3)),
            pltpu.SemaphoreType.DMA((3,)),
            pltpu.SemaphoreType.DMA((3,)),
            pltpu.SemaphoreType.DMA((16, 3)),
            pltpu.SemaphoreType.DMA((16, 3)),
            pltpu.SemaphoreType.DMA((20,)),
            pltpu.SemaphoreType.DMA((20,)),
        ],
        compiler_params=pltpu.CompilerParams(
            collective_id=0, has_side_effects=True, vmem_limit_bytes=24 * 1024 * 1024
        ),
        cost_estimate=pl.CostEstimate(
            flops=2 * 256 * 256 * 8192, bytes_accessed=1 << 20, transcendentals=0
        ),
    )(block_rows, block_cols, filled_count, tiles)


def solution(mesh):
    in_specs = (
        P("row", "col", None, None, None),
        P("row", "col", None),
        P("row", "col", None),
        P("row", "col"),
    )
    out_specs = P(("row", "layer"), "col")
    return jax.shard_map(local, mesh=mesh, in_specs=in_specs, out_specs=out_specs, check_vma=False)
```

time: 630 us -> 57.7 us (0.09)
  starting transfers between devices: 395 us -> 0 us
  waiting for transfers between devices: 166 us -> 0 us
  Pallas kernels: 0 us -> 54.6 us
  between operations: 18.6 us -> 0.68 us
  local copies, waits for them, and re-layouts: 19.4 us -> 2.25 us
  matrix products: 16.7 us -> 0 us
  other arithmetic: 11 us -> 0 us
    ppermute x92 -> x0, starting transfers between devices: 395 us -> none  [from_behind(): return lax.ppermute(block, axis, route)]
    reduce_scatter x1 -> x0, waiting for transfers between devices: 88.8 us -> none  [local(): lax.psum_scatter(partial_block, 'layer', scatter_dimension=0, tiled=True)]
    ppermute x92 -> x0, waiting for transfers between devices: 77.5 us -> none  [from_behind(): return lax.ppermute(block, axis, route)]
    pallas_call x0 -> x1, Pallas kernels: none -> 54.6 us  [local(): pl.pallas_call(kernel, out_shape=jax.ShapeDtypeStruct((2 * TILE, 2 * TILE...]
    dot_general x24 -> x0, matrix products: 16.7 us -> none  [the longest x8 8.29 us: add_dense(): jnp.einsum('si,sxz->ixz', routing, partial_rows, precision=lax.Precision....]
  transfers between devices with their start and end apart: 93 -> 0, of which waited for: 46 -> 0; matrix products, arithmetic and copies ran while one was open for 6% -> 0% of each run, Pallas kernels for 0% -> 0%
where the time goes in v1:
time: 57.7 us; the launch traced here: 57.6 us
  Pallas kernels  54.6 us (95%)
  local copies, waits for them, and re-layouts  2.25 us (4%)
  between operations  0.68 us (1%)
    pallas_call x1, Pallas kernels, local(): pl.pallas_call(kernel, out_shape=jax.ShapeDtypeStruct((2 * TILE, 2 * TILE...  54.6 us
    unnamed x7, local copies, waits for them, and re-layouts  2.25 us

profile of v1, /device:TPU:1, one launch (start us, length us, event | category | flops | bytes accessed | tf_op | source)
XLA Modules:
  0.0 57.6 jit_solution(12079254133341962602)
XLA Ops:
  0.7 0.0 copy-start.1
  0.7 0.0 copy-start.2
  0.7 0.6 %copy-done.1 = s32[1,1,3]{2,1,0:T(1,128)S(1)} copy-done((s32[1,1,3]{2,1,0:T(1,128)S(1)}, s32[1,1,3]{2,1,0:T(1,128)}, u32[]{:S(2)}) %copy-start.1) | copy-done | bytes 36
  1.3 0.0 copy-done.2
  1.3 0.0 copy-start
  1.3 0.9 %copy-done = bf16[1,1,3,128,128]{4,3,2,1,0:T(8,128)(2,1)S(1)} copy-done((bf16[1,1,3,128,128]{4,3,2,1,0:T(8,128)(2,1)S(1)}, bf16[1,1,3,128,128]{4,3,2,1,0:T(8,128)(2,1)}, u32[]{:S(2)}) %copy-start) | copy-done | bytes 98328
  2.2 54.6 %shard_map.46 = f32[256,256]{1,0:T(8,128)S(1)} custom-call(s32[1,1,3]{2,1,0:T(1,128)S(1)} %copy-done.1, s32[1,1,3]{2,1,0:T(1,128)S(1)} %copy-done.2, s32[1,1]{1,0:T(1,128)S(6)} %copy.6.count_ref, bf16[384,128]{1,0:T(8,128)(2,1)S(1)} %bitcast.1), custom_call_target="tpu_custom_call" | custom-call | flops 1073741824 | bytes 1048576 | tf_op jit(solution)/shard_map/pallas_call | solution.py:238
  56.9 0.7 %copy.7 = f32[256,256]{1,0:T(8,128)} copy(f32[256,256]{1,0:T(8,128)S(1)} %shard_map.46) | data formatting | bytes 524288
Async XLA Ops:
  0.7 0.7 %copy-start.1 = (s32[1,1,3]{2,1,0:T(1,128)S(1)}, s32[1,1,3]{2,1,0:T(1,128)}, u32[]{:S(2)}) copy-start(s32[1,1,3]{2,1,0:T(1,128)} %rows_ref.1) | copy-start | bytes 40
  0.7 0.7 %copy-start.2 = (s32[1,1,3]{2,1,0:T(1,128)S(1)}, s32[1,1,3]{2,1,0:T(1,128)}, u32[]{:S(2)}) copy-start(s32[1,1,3]{2,1,0:T(1,128)} %cols_ref.1) | copy-start | bytes 40
  1.3 0.9 %copy-start = (bf16[1,1,3,128,128]{4,3,2,1,0:T(8,128)(2,1)S(1)}, bf16[1,1,3,128,128]{4,3,2,1,0:T(8,128)(2,1)}, u32[]{:S(2)}) copy-start(bf16[1,1,3,128,128]{4,3,2,1,0:T(8,128)(2,1)} %param.4) | copy-start | bytes 294916

commit v2 on v0

v2 whole, which is shorter than its diff:
```python
import functools

import jax
import jax.numpy as jnp
from jax import lax
from jax.experimental import pallas as pl
from jax.experimental.pallas import tpu as pltpu
from jax.sharding import PartitionSpec as P

TILE = 128
SLOTS = 3
NX, NY, NZ = 4, 8, 16
Y_LO = 4
N_ROW = 16
N_COL = 32
MARK = 16
ROWS = SLOTS * TILE + MARK
CHUNKS = ((0, 128), (128, 128), (256, 144))
PIECES = len(CHUNKS)
FIRST, SECOND, WHOLE = (0, 208), (208, 192), (0, ROWS)
MESH = pl.DeviceIdType.MESH
ONWARD = {0: (1,), 1: (1,), 2: (1,), 3: (1,), 4: (1,), 5: (1,), 6: (1,), 7: (1,)}
ORDER = (1, 2, 3, 4, 5, 6, 7)
SENT = sum(2 for d, hops in ONWARD.items() for h in hops)
REACH = sorted({h for hops in ONWARD.values() for h in hops})
WORK = {4: (0, 1), 5: (2, 3, 4), 6: (5, 6, 7), 7: (8,)}
EARLY = 6


def kernel(
    tiles_ref, rows_ref, cols_ref, count_ref, out_ref,
    left, right, rows_s, cols_s, count_s, own_sem,
    left_s, ring_r, far_r, twin_r, right_s, right_r,
):
    row = lax.axis_index("row")
    col = lax.axis_index("col")
    layer = lax.axis_index("layer")
    x, y = row // Y_LO, layer * Y_LO + row % Y_LO
    z, core = col // 2, col % 2
    other = 1 - core
    away = 1 - 2 * core
    def at_xy(axis, way):
        def make():
            on_x = other if axis == 0 else core
            nx = lax.rem(x + way * on_x + NX, NX)
            ny = lax.rem(y + way * (1 - on_x) + NY, NY)
            return (nx * Y_LO + lax.rem(ny, Y_LO), col, ny // Y_LO)

        return make()

    def right_slot(f, g):
        f, g = (2 if f == -2 else f), (2 if g == -2 else g)

        def make():
            cx = lax.rem(x + f * other + g * core + NX, NX)
            cy = lax.rem(y + f * core + g * other + NY, Y_LO)
            return cx * Y_LO + cy

        return make()

    def remote(ref, slot, span, send, recv, device):
        part = ref.at[slot, pl.ds(span[0], span[1])]
        return pltpu.make_async_remote_copy(
            src_ref=part, dst_ref=part, send_sem=send, recv_sem=recv,
            device_id=device, device_id_type=MESH,
        )

    twin = (row, z * 2 + other, layer)

    def source(dist):
        return lax.rem(z - dist * away + NZ, NZ)

    def chip_on(hops):
        return lax.rem(z + hops * away + NZ, NZ)

    def first(way, hops, k):
        chip = lax.rem(z + way * hops + NZ, NZ)
        device = (row, chip * 2 + (0 if way > 0 else 1), layer)
        return remote(left, z * 2 + core, CHUNKS[k], left_s.at[0], ring_r.at[hops - 1, core, k], device)

    def ring(dist, hops, q, k):
        slot, device = source(dist) * 2 + q, (row, chip_on(hops) * 2 + core, layer)
        return remote(left, slot, CHUNKS[k], left_s.at[0], ring_r.at[dist + hops - 1, q, k], device)

    def ring_in(dist, q, k):
        return remote(left, source(dist) * 2 + q, CHUNKS[k], left_s.at[0], ring_r.at[dist - 1, q, k], twin)

    def far(i, k, hops=0):
        slot = source(8 - hops) * 2 + (other if i and not hops else core)
        device = (row, chip_on(hops) * 2 + (other if i else core), layer)
        return remote(left, slot, CHUNKS[k], left_s.at[0], far_r.at[i, k], device)

    def to_twin(dist, q, arrived=False):
        chip = lax.rem(z + dist * away + NZ, NZ) if arrived else source(dist)
        return remote(left, chip * 2 + q, WHOLE, left_s.at[1], twin_r.at[dist, q], twin)

    def own_to_twin(arrived=False):
        return remote(left, z * 2 + (other if arrived else core), WHOLE, left_s.at[1], twin_r.at[0, 0], twin)

    moves = []
    for axis, fs in ((0, (0,)), (1, (0, -1, 1, 2))):
        for f in fs:
            moves += [(f, 0, span, axis, way) for span, way in ((WHOLE, 1), (WHOLE, -1), (FIRST, 2), (SECOND, -2))]

    def along(n, arrived=False):
        f, g, span, axis, way = moves[n]
        if arrived:
            f, g = (f - way, g) if axis == 0 else (f, g - way)
        return remote(right, right_slot(f, g), span, right_s.at[0], right_r.at[n], at_xy(axis, way))

    def go(*numbers):
        for n in numbers:
            along(n).start()

    def come(*numbers):
        for n in numbers:
            along(n, True).wait_recv()

    def picked(ref, slot, codes):
        marks = ref[slot, pl.ds(SLOTS * TILE, MARK), :].astype(jnp.float32)
        tiles = [ref[slot, pl.ds(s * TILE, TILE), :] for s in range(SLOTS)]
        blocks = []
        for code in codes:
            total = None
            for s in range(SLOTS):
                hit = jnp.where(marks[s:s + 1, :] == code, 1.0, 0.0).astype(jnp.bfloat16)
                term = tiles[s] * hit
                total = term if total is None else total + term
            blocks.append(total)
        top, low = jnp.concatenate(blocks[:2], axis=1), jnp.concatenate(blocks[2:], axis=1)
        return jnp.concatenate([top, low], axis=0)

    base = (4 * layer).astype(jnp.float32)

    def add(r):
        for q in range(2):
            lhs = picked(left, r * 2 + q, [base + i for i in range(4)])
            rhs = picked(right, r, [float(4 * q + i) for i in range(4)])
            out_ref[...] += jnp.dot(lhs, rhs, preferred_element_type=jnp.float32)

    def add_steps(*dists):
        for dist in dists:
            if dist == 0:
                own_to_twin(True).wait_recv()
            elif dist < 8:
                to_twin(dist, 0, True).wait_recv()
                to_twin(dist, 1, True).wait_recv()
            if dist in (0, 8):
                add(source(dist))
            else:
                def body(i, carry):
                    add(lax.rem(z + dist * (2 * i - 1) + NZ, NZ))
                    return carry

                lax.fori_loop(0, 2, body, 0)

    barrier = pltpu.get_barrier_semaphore()
    greeted = [twin]
    for h in REACH:
        greeted += [(row, lax.rem(z + w * h + NZ, NZ) * 2 + c, layer) for w in (1, -1) for c in (0, 1)]
    greeted += [at_xy(axis, way) for axis in (0, 1) for way in (1, -1, 2, -2)]
    for device in greeted:
        pl.semaphore_signal(barrier, inc=1, device_id=device, device_id_type=MESH)
    own = [
        pltpu.make_async_copy(rows_ref, rows_s, own_sem.at[0]),
        pltpu.make_async_copy(cols_ref, cols_s, own_sem.at[1]),
        pltpu.make_async_copy(count_ref, count_s, own_sem.at[2]),
        pltpu.make_async_copy(tiles_ref, left.at[z * 2 + core, pl.ds(0, SLOTS * TILE)], own_sem.at[3]),
        pltpu.make_async_copy(tiles_ref, right.at[right_slot(0, 0), pl.ds(0, SLOTS * TILE)], own_sem.at[4]),
    ]
    for copy in own:
        copy.start()
    for copy in own[:3]:
        copy.wait()
    place = lax.broadcasted_iota(jnp.int32, (MARK, TILE), 0)
    marks = jnp.full((MARK, TILE), -1.0, jnp.float32)
    for s in range(SLOTS):
        code = jnp.where(s < count_s[0, 0], rows_s[0, 0, s] * 2 + cols_s[0, 0, s], -1)
        marks = jnp.where(place == s, code.astype(jnp.float32), marks)
    marks = marks.astype(jnp.bfloat16)
    left[z * 2 + core, pl.ds(SLOTS * TILE, MARK), :] = marks
    right[right_slot(0, 0), pl.ds(SLOTS * TILE, MARK), :] = marks
    for copy in own[3:]:
        copy.wait()
    pl.semaphore_wait(barrier, len(greeted))

    for hops in ONWARD[0]:
        for k in range(PIECES):
            first(1, hops, k).start()
            first(-1, hops, k).start()
    go(*range(4))
    own_to_twin().start()
    out_ref[...] = jnp.zeros_like(out_ref)

    def panel(step):
        if step == 0:
            go(*range(4, 8))
        elif step == 1:
            come(0)
            go(*range(8, 12))
            come(1)
            go(*range(12, 16))
        else:
            come(2, 3)
            go(*range(16, 20))

    panel_first = jnp.logical_and(z >= 1, z < 5)

    @pl.when(panel_first)
    def _():
        for step in range(3):
            panel(step)


    for step, d in enumerate(ORDER):
        for k in range(PIECES):
            for hops in ONWARD.get(d, ()):
                for q in range(2):
                    if hops == ONWARD[d][0]:
                        ring_in(d, q, k).wait_recv()
                    if d + hops < 8:
                        ring(d, hops, q, k).start()
                if d + hops == 8:
                    far(0, k, hops).start()
                    far(1, k, hops).start()
            if d not in ONWARD:
                for q in range(2):
                    ring_in(d, q, k).wait_recv()
        to_twin(d, 0).start()
        to_twin(d, 1).start()
        if step < 3:
            pl.when(jnp.logical_not(panel_first))(functools.partial(panel, step))
        if step in WORK:

            @pl.when(z < EARLY)
            def _(step=step):
                if step == 4:
                    come(*range(4, 20))
                add_steps(*WORK[step])

    for k in range(PIECES):
        for i in range(2):
            far(i, k).wait_recv()

    @pl.when(z < EARLY)
    def _():
        add_steps(*WORK[7])

    @pl.when(z >= EARLY)
    def _():
        come(*range(4, 20))
        own_to_twin(True).wait_recv()
        for dist in range(1, 8):
            for q in range(2):
                to_twin(dist, q, True).wait_recv()

        def body(i, carry):
            add(i)
            return carry

        lax.fori_loop(0, N_ROW, body, 0)

    for i, cells in ((0, SENT), (1, 15)):
        sent = left.at[pl.ds(0, cells)]
        pltpu.make_async_copy(sent, sent, left_s.at[i]).wait()
    sent = right.at[pl.ds(0, 15)]
    pltpu.make_async_copy(sent, sent, right_s.at[0]).wait()


def local(tile_data, block_rows, block_cols, filled_count):
    tiles = tile_data.reshape(SLOTS * TILE, TILE)
    hbm = pl.BlockSpec(memory_space=pltpu.HBM)
    return pl.pallas_call(
        kernel,
        out_shape=jax.ShapeDtypeStruct((2 * TILE, 2 * TILE), jnp.float32),
        in_specs=[hbm, hbm, hbm, hbm],
        out_specs=pl.BlockSpec(memory_space=pltpu.VMEM),
        scratch_shapes=[
            pltpu.VMEM((N_COL, ROWS, TILE), jnp.bfloat16),
            pltpu.VMEM((N_ROW, ROWS, TILE), jnp.bfloat16),
            pltpu.SMEM((1, 1, SLOTS), jnp.int32),
            pltpu.SMEM((1, 1, SLOTS), jnp.int32),
            pltpu.SMEM((1, 1), jnp.int32),
            pltpu.SemaphoreType.DMA((5,)),
            pltpu.SemaphoreType.DMA((2,)),
            pltpu.SemaphoreType.DMA((7, 2, PIECES)),
            pltpu.SemaphoreType.DMA((2, PIECES)),
            pltpu.SemaphoreType.DMA((8, 2)),
            pltpu.SemaphoreType.DMA((1,)),
            pltpu.SemaphoreType.DMA((20,)),
        ],
        compiler_params=pltpu.CompilerParams(
            collective_id=0, has_side_effects=True, vmem_limit_bytes=24 * 1024 * 1024
        ),
        cost_estimate=pl.CostEstimate(
            flops=2 * 256 * 256 * 8192, bytes_accessed=1 << 20, transcendentals=0
        ),
    )(tiles, block_rows, block_cols, filled_count)


def solution(mesh):
    in_specs = (
        P("row", "col", None, None, None),
        P("row", "col", None),
        P("row", "col", None),
        P("row", "col"),
    )
    out_specs = P(("row", "layer"), "col")
    return jax.shard_map(local, mesh=mesh, in_specs=in_specs, out_specs=out_specs, check_vma=False)
```

time: 630 us -> 49.4 us (0.08)
  the two profiles are of different devices: /device:TPU:1 before, /device:TPU:65 now
where the time goes in v2:
time: 49.4 us; the launch traced here: 49.2 us
  Pallas kernels  46.3 us (94%)
  local copies, waits for them, and re-layouts  2.25 us (5%)
  between operations  0.68 us (1%)
    pallas_call x1, Pallas kernels, local(): pl.pallas_call(kernel, out_shape=jax.ShapeDtypeStruct((2 * TILE, 2 * TILE...  46.3 us
    unnamed x7, local copies, waits for them, and re-layouts  2.25 us

profile of v2, /device:TPU:65, one launch (start us, length us, event | category | flops | bytes accessed | tf_op | source)
XLA Modules:
  0.0 49.2 jit_solution(2733067370196641184)
XLA Ops:
  0.7 0.0 copy-start.1
  0.7 0.0 copy-start.2
  0.7 0.6 %copy-done.1 = s32[1,1,3]{2,1,0:T(1,128)S(1)} copy-done((s32[1,1,3]{2,1,0:T(1,128)S(1)}, s32[1,1,3]{2,1,0:T(1,128)}, u32[]{:S(2)}) %copy-start.1) | copy-done | bytes 36
  1.3 0.0 copy-done.2
  1.3 0.0 copy-start
  1.3 0.9 %copy-done = bf16[1,1,3,128,128]{4,3,2,1,0:T(8,128)(2,1)S(1)} copy-done((bf16[1,1,3,128,128]{4,3,2,1,0:T(8,128)(2,1)S(1)}, bf16[1,1,3,128,128]{4,3,2,1,0:T(8,128)(2,1)}, u32[]{:S(2)}) %copy-start) | copy-done | bytes 98328
  2.2 46.3 %shard_map.46 = f32[256,256]{1,0:T(8,128)S(1)} custom-call(bf16[384,128]{1,0:T(8,128)(2,1)S(1)} %bitcast.1, s32[1,1,3]{2,1,0:T(1,128)S(1)} %copy-done.1, s32[1,1,3]{2,1,0:T(1,128)S(1)} %copy-done.2, s32[1,1]{1,0:T(1,128)S(6)} %copy.6.count_ref), custom_call_target="tpu_custom_call" | custom-call | flops 1073741824 | bytes 1048576 | tf_op jit(solution)/shard_map/pallas_call | solution.py:273
  48.5 0.7 %copy.7 = f32[256,256]{1,0:T(8,128)} copy(f32[256,256]{1,0:T(8,128)S(1)} %shard_map.46) | data formatting | bytes 524288
Async XLA Ops:
  0.7 0.7 %copy-start.1 = (s32[1,1,3]{2,1,0:T(1,128)S(1)}, s32[1,1,3]{2,1,0:T(1,128)}, u32[]{:S(2)}) copy-start(s32[1,1,3]{2,1,0:T(1,128)} %rows_ref.1) | copy-start | bytes 40
  0.7 0.7 %copy-start.2 = (s32[1,1,3]{2,1,0:T(1,128)S(1)}, s32[1,1,3]{2,1,0:T(1,128)}, u32[]{:S(2)}) copy-start(s32[1,1,3]{2,1,0:T(1,128)} %cols_ref.1) | copy-start | bytes 40
  1.3 0.9 %copy-start = (bf16[1,1,3,128,128]{4,3,2,1,0:T(8,128)(2,1)S(1)}, bf16[1,1,3,128,128]{4,3,2,1,0:T(8,128)(2,1)}, u32[]{:S(2)}) copy-start(bf16[1,1,3,128,128]{4,3,2,1,0:T(8,128)(2,1)} %param.4) | copy-start | bytes 294916

commit v3 on v2

--- a/solution.py
+++ b/solution.py
@@ -22,15 +22,18 @@
 ONWARD = {0: (1,), 1: (1,), 2: (1,), 3: (1,), 4: (1,), 5: (1,), 6: (1,), 7: (1,)}
 ORDER = (1, 2, 3, 4, 5, 6, 7)
 SENT = sum(2 for d, hops in ONWARD.items() for h in hops)
+EXPRESS = (8, 9)
+HUB = 7
+PASS_ON = 5
 REACH = sorted({h for hops in ONWARD.values() for h in hops})
-WORK = {4: (0, 1), 5: (2, 3, 4), 6: (5, 6, 7), 7: (8,)}
+WORK = {5: (0, 1, 2, 3), 6: (4, 5, 6, 7), 7: (8,)}
 EARLY = 6
 
 
 def kernel(
     tiles_ref, rows_ref, cols_ref, count_ref, out_ref,
     left, right, rows_s, cols_s, count_s, own_sem,
-    left_s, ring_r, far_r, twin_r, right_s, right_r,
+    left_s, ring_r, far_r, twin_r, express_r, right_s, right_r,
 ):
     row = lax.axis_index("row")
     col = lax.axis_index("col")
@@ -94,6 +97,20 @@
         chip = lax.rem(z + dist * away + NZ, NZ) if arrived else source(dist)
         return remote(left, chip * 2 + q, WHOLE, left_s.at[1], twin_r.at[dist, q], twin)
 
+    zero_up = jnp.logical_and(z == 0, core == 0)
+    zero_down = jnp.logical_and(z == 0, core == 1)
+    before_zero = jnp.logical_and(z == NZ - 1, core == 0)
+    after_zero = jnp.logical_and(z == 1, core == 1)
+
+    def express(i, q):
+        return remote(left, EXPRESS[i] * 2 + q, WHOLE, left_s.at[2], express_r.at[i, q], (row, 1, layer))
+
+    def express_on(i, q):
+        return remote(left, EXPRESS[i] * 2 + q, WHOLE, left_s.at[1], express_r.at[i, q], (row, 0, layer))
+
+    hub = jnp.logical_and(z == HUB, core == 1)
+    parcels = [(i, q) for i in range(len(EXPRESS)) for q in range(2)]
+
     def own_to_twin(arrived=False):
         return remote(left, z * 2 + (other if arrived else core), WHOLE, left_s.at[1], twin_r.at[0, 0], twin)
 
@@ -117,15 +134,14 @@
             along(n, True).wait_recv()
 
     def picked(ref, slot, codes):
-        marks = ref[slot, pl.ds(SLOTS * TILE, MARK), :].astype(jnp.float32)
+        marks = ref[slot, pl.ds(SLOTS * TILE, MARK), :]
+        wide = [jnp.broadcast_to(marks[s:s + 1, :], (TILE, TILE)) for s in range(SLOTS)]
         tiles = [ref[slot, pl.ds(s * TILE, TILE), :] for s in range(SLOTS)]
         blocks = []
         for code in codes:
-            total = None
+            total = jnp.zeros((TILE, TILE), jnp.bfloat16)
             for s in range(SLOTS):
-                hit = jnp.where(marks[s:s + 1, :] == code, 1.0, 0.0).astype(jnp.bfloat16)
-                term = tiles[s] * hit
-                total = term if total is None else total + term
+                total = jnp.where(wide[s] == jnp.asarray(code, jnp.bfloat16), tiles[s], total)
             blocks.append(total)
         top, low = jnp.concatenate(blocks[:2], axis=1), jnp.concatenate(blocks[2:], axis=1)
         return jnp.concatenate([top, low], axis=0)
@@ -143,8 +159,14 @@
             if dist == 0:
                 own_to_twin(True).wait_recv()
             elif dist < 8:
-                to_twin(dist, 0, True).wait_recv()
-                to_twin(dist, 1, True).wait_recv()
+                def other_way(dist=dist):
+                    to_twin(dist, 0, True).wait_recv()
+                    to_twin(dist, 1, True).wait_recv()
+
+                if dist == 7:
+                    pl.when(jnp.logical_not(zero_down))(other_way)
+                else:
+                    other_way()
             if dist in (0, 8):
                 add(source(dist))
             else:
@@ -161,6 +183,11 @@
     greeted += [at_xy(axis, way) for axis in (0, 1) for way in (1, -1, 2, -2)]
     for device in greeted:
         pl.semaphore_signal(barrier, inc=1, device_id=device, device_id_type=MESH)
+    @pl.when(zero_down)
+    def _():
+        peer = (row, HUB * 2 + 1, layer)
+        pl.semaphore_signal(barrier, inc=1, device_id=peer, device_id_type=MESH)
+
     own = [
         pltpu.make_async_copy(rows_ref, rows_s, own_sem.at[0]),
         pltpu.make_async_copy(cols_ref, cols_s, own_sem.at[1]),
@@ -182,7 +209,7 @@
     right[right_slot(0, 0), pl.ds(SLOTS * TILE, MARK), :] = marks
     for copy in own[3:]:
         copy.wait()
-    pl.semaphore_wait(barrier, len(greeted))
+    pl.semaphore_wait(barrier, len(greeted) + jnp.where(hub, 1, 0))
 
     for hops in ONWARD[0]:
         for k in range(PIECES):
@@ -212,35 +239,70 @@
             panel(step)
 
 
+    def last_ring():
+        for k in range(PIECES):
+            for q in range(2):
+                ring_in(7, q, k).wait_recv()
+
+            @pl.when(jnp.logical_not(jnp.logical_or(before_zero, after_zero)))
+            def _(k=k):
+                far(0, k, 1).start()
+                far(1, k, 1).start()
+
+        to_twin(7, 0).start()
+        to_twin(7, 1).start()
+
+    def last_zero():
+        for i, q in parcels:
+            express_on(i, q).wait_recv()
+        for k in range(PIECES):
+            far(0, k, 1).start()
+            far(1, k, 1).start()
+
     for step, d in enumerate(ORDER):
-        for k in range(PIECES):
-            for hops in ONWARD.get(d, ()):
-                for q in range(2):
-                    if hops == ONWARD[d][0]:
-                        ring_in(d, q, k).wait_recv()
-                    if d + hops < 8:
-                        ring(d, hops, q, k).start()
-                if d + hops == 8:
-                    far(0, k, hops).start()
-                    far(1, k, hops).start()
-            if d not in ONWARD:
+        if d == 7:
+            pl.when(jnp.logical_not(zero_up))(last_ring)
+            pl.when(zero_up)(last_zero)
+        else:
+            for k in range(PIECES):
                 for q in range(2):
                     ring_in(d, q, k).wait_recv()
-        to_twin(d, 0).start()
-        to_twin(d, 1).start()
+                    if d == 6:
+                        pl.when(jnp.logical_not(before_zero))(ring(d, 1, q, k).start)
+                    else:
+                        ring(d, 1, q, k).start()
+            to_twin(d, 0).start()
+            to_twin(d, 1).start()
+        if 1 <= d <= len(EXPRESS):
+
+            @pl.when(hub)
+            def _(i=d - 1):
+                for q in range(2):
+                    express(i, q).start()
+
+        if d == PASS_ON:
+
+            @pl.when(zero_down)
+            def _():
+                for i, q in parcels:
+                    express(i, q).wait_recv()
+                    express_on(i, q).start()
+
         if step < 3:
             pl.when(jnp.logical_not(panel_first))(functools.partial(panel, step))
         if step in WORK:
 
             @pl.when(z < EARLY)
             def _(step=step):
-                if step == 4:
+                if step == 5:
                     come(*range(4, 20))
                 add_steps(*WORK[step])
 
-    for k in range(PIECES):
-        for i in range(2):
-            far(i, k).wait_recv()
+    @pl.when(z != 0)
+    def _():
+        for k in range(PIECES):
+            for i in range(2):
+                far(i, k).wait_recv()
 
     @pl.when(z < EARLY)
     def _():
@@ -260,9 +322,18 @@
 
         lax.fori_loop(0, N_ROW, body, 0)
 
-    for i, cells in ((0, SENT), (1, 15)):
+    def left_by(i, cells):
         sent = left.at[pl.ds(0, cells)]
         pltpu.make_async_copy(sent, sent, left_s.at[i]).wait()
+
+    usual = jnp.logical_not(jnp.logical_or(before_zero, after_zero))
+    pl.when(usual)(lambda: left_by(0, SENT))
+    pl.when(before_zero)(lambda: left_by(0, SENT - 4))
+    pl.when(after_zero)(lambda: left_by(0, SENT - 2))
+    pl.when(z != 0)(lambda: left_by(1, 15))
+    pl.when(zero_down)(lambda: left_by(1, 15 + len(parcels)))
+    pl.when(zero_up)(lambda: left_by(1, 13))
+    pl.when(hub)(lambda: left_by(2, len(parcels)))
     sent = right.at[pl.ds(0, 15)]
     pltpu.make_async_copy(sent, sent, right_s.at[0]).wait()
 
@@ -282,10 +353,11 @@
             pltpu.SMEM((1, 1, SLOTS), jnp.int32),
             pltpu.SMEM((1, 1), jnp.int32),
             pltpu.SemaphoreType.DMA((5,)),
-            pltpu.SemaphoreType.DMA((2,)),
+            pltpu.SemaphoreType.DMA((3,)),
             pltpu.SemaphoreType.DMA((7, 2, PIECES)),
             pltpu.SemaphoreType.DMA((2, PIECES)),
             pltpu.SemaphoreType.DMA((8, 2)),
+            pltpu.SemaphoreType.DMA((len(EXPRESS), 2)),
             pltpu.SemaphoreType.DMA((1,)),
             pltpu.SemaphoreType.DMA((20,)),
         ],

time: 49.4 us -> 48.2 us (0.976)
  Pallas kernels: 46.3 us -> 45.1 us
    pallas_call x1, Pallas kernels: 46.3 us -> 45.1 us  [local(): pl.pallas_call(kernel, out_shape=jax.ShapeDtypeStruct((2 * TILE, 2 * TILE...]
where the time goes in v3:
time: 48.2 us; the launch traced here: 48.1 us
  Pallas kernels  45.1 us (94%)
  local copies, waits for them, and re-layouts  2.25 us (5%)
  between operations  0.68 us (1%)
    pallas_call x1, Pallas kernels, local(): pl.pallas_call(kernel, out_shape=jax.ShapeDtypeStruct((2 * TILE, 2 * TILE...  45.1 us
    unnamed x7, local copies, waits for them, and re-layouts  2.25 us

profile of v3, /device:TPU:65, one launch (start us, length us, event | category | flops | bytes accessed | tf_op | source)
XLA Modules:
  0.0 48.1 jit_solution(6907653838844854821)
XLA Ops:
  0.7 0.0 copy-start.1
  0.7 0.0 copy-start.2
  0.7 0.6 %copy-done.1 = s32[1,1,3]{2,1,0:T(1,128)S(1)} copy-done((s32[1,1,3]{2,1,0:T(1,128)S(1)}, s32[1,1,3]{2,1,0:T(1,128)}, u32[]{:S(2)}) %copy-start.1) | copy-done | bytes 36
  1.3 0.0 copy-done.2
  1.3 0.0 copy-start
  1.3 0.9 %copy-done = bf16[1,1,3,128,128]{4,3,2,1,0:T(8,128)(2,1)S(1)} copy-done((bf16[1,1,3,128,128]{4,3,2,1,0:T(8,128)(2,1)S(1)}, bf16[1,1,3,128,128]{4,3,2,1,0:T(8,128)(2,1)}, u32[]{:S(2)}) %copy-start) | copy-done | bytes 98328
  2.2 45.1 %shard_map.46 = f32[256,256]{1,0:T(8,128)S(1)} custom-call(bf16[384,128]{1,0:T(8,128)(2,1)S(1)} %bitcast.1, s32[1,1,3]{2,1,0:T(1,128)S(1)} %copy-done.1, s32[1,1,3]{2,1,0:T(1,128)S(1)} %copy-done.2, s32[1,1]{1,0:T(1,128)S(6)} %copy.6.count_ref), custom_call_target="tpu_custom_call" | custom-call | flops 1073741824 | bytes 1048576 | tf_op jit(solution)/shard_map/pallas_call | solution.py:344
  47.3 0.7 %copy.7 = f32[256,256]{1,0:T(8,128)} copy(f32[256,256]{1,0:T(8,128)S(1)} %shard_map.46) | data formatting | bytes 524288
Async XLA Ops:
  0.7 0.7 %copy-start.1 = (s32[1,1,3]{2,1,0:T(1,128)S(1)}, s32[1,1,3]{2,1,0:T(1,128)}, u32[]{:S(2)}) copy-start(s32[1,1,3]{2,1,0:T(1,128)} %rows_ref.1) | copy-start | bytes 40
  0.7 0.7 %copy-start.2 = (s32[1,1,3]{2,1,0:T(1,128)S(1)}, s32[1,1,3]{2,1,0:T(1,128)}, u32[]{:S(2)}) copy-start(s32[1,1,3]{2,1,0:T(1,128)} %cols_ref.1) | copy-start | bytes 40
  1.3 0.9 %copy-start = (bf16[1,1,3,128,128]{4,3,2,1,0:T(8,128)(2,1)S(1)}, bf16[1,1,3,128,128]{4,3,2,1,0:T(8,128)(2,1)}, u32[]{:S(2)}) copy-start(bf16[1,1,3,128,128]{4,3,2,1,0:T(8,128)(2,1)} %param.4) | copy-start | bytes 294916

commit v4 on v3

--- a/solution.py
+++ b/solution.py
@@ -26,7 +26,7 @@
 HUB = 7
 PASS_ON = 5
 REACH = sorted({h for hops in ONWARD.values() for h in hops})
-WORK = {5: (0, 1, 2, 3), 6: (4, 5, 6, 7), 7: (8,)}
+WORK = {5: (0, 1, 2), 6: (3, 4, 5, 6, 7), 7: (8,)}
 EARLY = 6
 
 

time: 48.2 us -> 47.7 us (0.990)
  Pallas kernels: 45.1 us -> 44.6 us
    pallas_call x1, Pallas kernels: 45.1 us -> 44.6 us  [local(): pl.pallas_call(kernel, out_shape=jax.ShapeDtypeStruct((2 * TILE, 2 * TILE...]
where the time goes in v4:
time: 47.7 us; the launch traced here: 47.6 us
  Pallas kernels  44.6 us (94%)
  local copies, waits for them, and re-layouts  2.25 us (5%)
  between operations  0.68 us (1%)
    pallas_call x1, Pallas kernels, local(): pl.pallas_call(kernel, out_shape=jax.ShapeDtypeStruct((2 * TILE, 2 * TILE...  44.6 us
    unnamed x7, local copies, waits for them, and re-layouts  2.25 us

profile of v4, /device:TPU:65, one launch (start us, length us, event | category | flops | bytes accessed | tf_op | source)
XLA Modules:
  0.0 47.6 jit_solution(4221109853713246190)
XLA Ops:
  0.7 0.0 copy-start.1
  0.7 0.0 copy-start.2
  0.7 0.6 %copy-done.1 = s32[1,1,3]{2,1,0:T(1,128)S(1)} copy-done((s32[1,1,3]{2,1,0:T(1,128)S(1)}, s32[1,1,3]{2,1,0:T(1,128)}, u32[]{:S(2)}) %copy-start.1) | copy-done | bytes 36
  1.3 0.0 copy-done.2
  1.3 0.0 copy-start
  1.3 0.9 %copy-done = bf16[1,1,3,128,128]{4,3,2,1,0:T(8,128)(2,1)S(1)} copy-done((bf16[1,1,3,128,128]{4,3,2,1,0:T(8,128)(2,1)S(1)}, bf16[1,1,3,128,128]{4,3,2,1,0:T(8,128)(2,1)}, u32[]{:S(2)}) %copy-start) | copy-done | bytes 98328
  2.2 44.6 %shard_map.46 = f32[256,256]{1,0:T(8,128)S(1)} custom-call(bf16[384,128]{1,0:T(8,128)(2,1)S(1)} %bitcast.1, s32[1,1,3]{2,1,0:T(1,128)S(1)} %copy-done.1, s32[1,1,3]{2,1,0:T(1,128)S(1)} %copy-done.2, s32[1,1]{1,0:T(1,128)S(6)} %copy.6.count_ref), custom_call_target="tpu_custom_call" | custom-call | flops 1073741824 | bytes 1048576 | tf_op jit(solution)/shard_map/pallas_call | solution.py:344
  46.8 0.7 %copy.7 = f32[256,256]{1,0:T(8,128)} copy(f32[256,256]{1,0:T(8,128)S(1)} %shard_map.46) | data formatting | bytes 524288
Async XLA Ops:
  0.7 0.7 %copy-start.1 = (s32[1,1,3]{2,1,0:T(1,128)S(1)}, s32[1,1,3]{2,1,0:T(1,128)}, u32[]{:S(2)}) copy-start(s32[1,1,3]{2,1,0:T(1,128)} %rows_ref.1) | copy-start | bytes 40
  0.7 0.7 %copy-start.2 = (s32[1,1,3]{2,1,0:T(1,128)S(1)}, s32[1,1,3]{2,1,0:T(1,128)}, u32[]{:S(2)}) copy-start(s32[1,1,3]{2,1,0:T(1,128)} %cols_ref.1) | copy-start | bytes 40
  1.3 0.9 %copy-start = (bf16[1,1,3,128,128]{4,3,2,1,0:T(8,128)(2,1)S(1)}, bf16[1,1,3,128,128]{4,3,2,1,0:T(8,128)(2,1)}, u32[]{:S(2)}) copy-start(bf16[1,1,3,128,128]{4,3,2,1,0:T(8,128)(2,1)} %param.4) | copy-start | bytes 294916
